TPU v7x, 256 devices: a whole 4x4x8 slice. The times are simulated.
256 devices in a mesh: tm: 8 (over z), spec: 32 (over x, y, core).
Axes of the slice: x: 4, y: 4, z: 8, core: 2. Of those that a mesh axis runs over, the one named last changes fastest.
Arguments:
- base_flow: float32 [8, 2048, 2048], P('tm', 'spec'), may hold values from -6 to 6
- tangents: float32 [8, 2, 2048, 2048], P('tm', None, 'spec'), as said below
- end_matrix: float32 [2, 2], replicated, may hold values from 0.5 to 1.5
Outputs:
- covariant_vectors: float32 [8, 2, 2048, 2048], P('tm', None, 'spec')
- evolved_basis: float32 [8, 2, 2048, 2048], P('tm', None, 'spec')
- coefficients: float32 [8, 2, 2], P('tm')
- growth: float32 [8, 2], P('tm')
Inputs may be any that keep to these rules, and one draw needn't show every extreme that they name: `tangents`: real values.
All inputs are finite; a program needn't handle non-finite values.
Results may differ from a plain program's by a relative error of at most 0.025.
Values sent between devices are 32-bit elements; how exact they have to be, the bound alone decides.
A program may use at most 128 MiB of HBM per device.

v0:
```python
import functools
import math

import jax
import jax.numpy as jnp
import ml_dtypes
import numpy as np
from jax import lax
from jax.experimental import pallas as pl
from jax.experimental.pallas import tpu as pltpu
from jax.sharding import PartitionSpec as P

NG = 2048
HALF = NG // 2
K = 2
SPEC = 32
TM = 8
SLAB = NG // SPEC
BAND = NG // 3
ROWS = 22
PAD = 24
LANES = 128
SIDE = 16 * 2 * PAD

time_step = 0.1
visc_scale = 15.0
MESH = pl.DeviceIdType.MESH
F32 = jnp.float32
BF16 = jnp.bfloat16


def row_tables():
    owner = np.arange(16)[:, None, None]
    part = np.arange(2)[None, :, None]
    row = np.arange(PAD)[None, None, :]
    y = np.arange(HALF)[None, :]
    tables = []
    for parity in range(2):
        wave = 2 * (ROWS * owner + row) + parity
        valid = np.broadcast_to((wave <= BAND) & (row < ROWS), (16, 2, PAD)).reshape(SIDE, 1)
        waves = np.broadcast_to(wave, (16, 2, PAD)).reshape(SIDE, 1)
        parts = np.broadcast_to(part, (16, 2, PAD)).reshape(SIDE, 1)
        angle = (waves * y % NG) * (2.0 * math.pi / NG)
        tables.append(np.where(valid, np.where(parts == 0, np.cos(angle), -np.sin(angle)), 0.0))
    return np.stack(tables)


def lane_tables():
    index = np.arange(SLAB)
    angle = (index[:, None] * index[None, :] % SLAB) * (2.0 * math.pi / SLAB)
    cos, sin, zero = np.cos(angle), np.sin(angle), np.zeros((SLAB, SLAB))
    pair_forward = np.block(
        [[cos, zero, -sin, zero], [zero, cos, zero, -sin], [sin, zero, cos, zero], [zero, sin, zero, cos]]
    )
    pair_inverse = np.block(
        [[cos, zero, sin, zero], [zero, cos, zero, sin], [-sin, zero, cos, zero], [zero, -sin, zero, cos]]
    )
    twice = []
    for half in range(2):
        real = pair_forward[:, half * SLAB : (half + 1) * SLAB]
        imag = pair_forward[:, (2 + half) * SLAB : (3 + half) * SLAB]
        twice.append(np.concatenate([imag, imag, -real, -real], axis=1))
    return np.stack([twice[0], twice[1], pair_forward, pair_inverse])


def twist_tables():
    first = np.arange(32)[:, None]
    place = (np.arange(LANES) % SLAB)[None, :]
    angle = (first * place) * (2.0 * math.pi / NG)
    return np.stack([np.cos(angle), np.sin(angle)])


def turned(re, im, angle):
    c, s = math.cos(angle), math.sin(angle)
    if abs(s) < 1e-9 and c > 0:
        return re, im
    if abs(c) < 1e-9:
        return (-im, re) if s > 0 else (im, -re)
    if abs(abs(c) - abs(s)) < 1e-9:
        root = math.sqrt(0.5)
        sc, ss = (root if c > 0 else -root), (root if s > 0 else -root)
        if sc == ss:
            return (re - im) * sc, (re + im) * sc
        return (re + im) * sc, (im - re) * sc
    return re * c - im * s, re * s + im * c


def short_transform(res, ims, sign):
    count = len(res)
    if count == 1:
        return res, ims
    er, ei = short_transform(res[0::2], ims[0::2], sign)
    dr, di = short_transform(res[1::2], ims[1::2], sign)
    half = count // 2
    out_r, out_i = [None] * count, [None] * count
    for k in range(half):
        tr, ti = turned(dr[k], di[k], sign * 2.0 * math.pi * k / count)
        out_r[k], out_i[k] = er[k] + tr, ei[k] + ti
        out_r[k + half], out_i[k + half] = er[k] - tr, ei[k] - ti
    return out_r, out_i


def dot(a, b):
    return jnp.dot(a, b, preferred_element_type=F32)


def kernel(
    base_ref,
    tang_ref,
    end_ref,
    tf_ref,
    ti_ref,
    lane_ref,
    twist_ref,
    cov_ref,
    basis_ref,
    coef_ref,
    growth_ref,
    s1,
    r1,
    s2,
    r2,
    s3,
    r3,
    s4,
    r4,
    gs,
    gr,
    ts,
    tr,
    tb,
    tt,
    tw,
    folded,
    zr,
    zi,
    mult_flow,
    mult_slope,
    mult_decay,
    base_flow,
    product,
    send_sem,
    recv_sem,
):
    me = lax.axis_index("spec")
    seg = lax.axis_index("tm")
    my_slot = lax.rem(me, 2) * 16 + me // 2
    low = lax.broadcasted_iota(jnp.int32, (1, LANES), 1) < SLAB

    barrier = pltpu.get_barrier_semaphore()

    def greet(d, carry):
        pl.semaphore_signal(barrier, inc=1, device_id={"spec": lax.rem(me + d, SPEC)}, device_id_type=MESH)
        return carry

    for ref in (r1, r2, r3, r4):
        lead = ref.shape[:-2]
        ref[(slice(None),) * len(lead) + (slice(16, 24), slice(None))] = jnp.zeros(lead + (8, LANES), F32)

    lax.fori_loop(1, SPEC, greet, 0)

    def greet_segment(d, carry):
        pl.semaphore_signal(barrier, inc=1, device_id={"tm": lax.rem(seg + d, TM)}, device_id_type=MESH)
        return carry

    lax.fori_loop(1, TM, greet_segment, 0)

    def send_all(phase, source, target):
        def step(d, carry):
            peer = lax.rem(me + d, SPEC)
            slot = lax.rem(peer, 2) * 16 + peer // 2
            pltpu.make_async_remote_copy(
                src_ref=source(peer, slot),
                dst_ref=target,
                send_sem=send_sem.at[phase],
                recv_sem=recv_sem.at[phase],
                device_id={"spec": peer},
                device_id_type=MESH,
            ).start()
            return carry

        lax.fori_loop(1, SPEC, step, 0)

    def wait_for(sem, phase, ref):
        pltpu.make_async_copy(ref, ref, sem.at[phase]).wait()

    some = pl.ds(0, ROWS)
    most = pl.ds(0, SPEC - 1)

    for parity in range(2):
        def fold(half_parity=parity):
            for index, ref in ((0, tang_ref.at[0, 0]), (1, tang_ref.at[0, 1]), (2, base_ref.at[0]), (3, base_ref.at[0])):
                lo, hi = ref[:, :HALF], ref[:, HALF:]
                value = lo + hi if half_parity == 0 else lo - hi
                folded[index * SLAB : (index + 1) * SLAB, :] = value.astype(BF16)

        fold()

        def spectrum_rows(step, carry, parity=parity):
            rows = pl.ds(pl.multiple_of(step * 192, 192), 192)
            out = lax.dot_general(
                tf_ref[parity, rows, :], folded[...], (((1,), (1,)), ((), ())), preferred_element_type=F32
            ).reshape(4, 2, PAD, 2 * LANES)
            slots = pl.ds(parity * 16 + step * 4, 4)
            s1[slots, 0] = jnp.where(low[None], out[:, 0, :, LANES:], out[:, 1, :, LANES:])
            s1[slots, 1] = out[:, 0, :, :LANES]
            s1[slots, 2] = out[:, 1, :, :LANES]
            return carry

        lax.fori_loop(0, 4, spectrum_rows, 0)

    pl.semaphore_wait(barrier, SPEC - 1 + TM - 1)
    send_all(0, lambda peer, slot: s1.at[slot, pl.ds(0, 1), some], r1.at[me, pl.ds(0, 1), some])
    send_all(1, lambda peer, slot: s1.at[slot, pl.ds(1, 2), some], r1.at[me, pl.ds(1, 2), some])
    r1[me] = s1[my_slot]

    lane = lax.broadcasted_iota(jnp.int32, (PAD, LANES), 1)
    row = lax.broadcasted_iota(jnp.int32, (PAD, LANES), 0)
    second = 2 * (ROWS * (me // 2) + row) + lax.rem(me, 2)
    second_keep = (second <= BAND) & (row < ROWS)
    second_wave = second.astype(F32)
    low_rows = lane < SLAB
    column = jnp.where(second == 0, 1.0, 2.0)
    to_field = column * (1.0 / float(NG * NG))
    gram_weight = jnp.where(second_keep, column * (1.0 / float(NG) ** 4), 0.0)

    def multipliers(k1, carry):
        first = k1 + 32 * lax.rem(lane, SLAB)
        first = jnp.where(first < HALF, first, first - NG)
        first_wave = first.astype(F32)
        keep = jnp.where(second_keep & (jnp.abs(first) <= BAND), 1.0, 0.0)
        square = first_wave * first_wave + second_wave * second_wave
        inverse = jnp.where(square > 0.0, 1.0 / jnp.maximum(square, 1.0), 0.0)
        decay = keep * jnp.exp(-(visc_scale / BAND**2) * time_step * square)
        mult_flow[k1] = keep * to_field * inverse * jnp.where(low_rows, -second_wave, first_wave)
        mult_decay[k1] = decay
        mult_slope[k1] = (time_step * decay) * jnp.where(
            low_rows,
            first_wave * first_wave - second_wave * second_wave,
            2.0 * first_wave * second_wave,
        )
        return carry

    lax.fori_loop(0, 32, multipliers, 0)

    def first_forward(load, target):
        def body(step, carry):
            rows = pl.ds(pl.multiple_of(step * 8, 8), 8)
            pairs = [load(i, rows) for i in range(SPEC)]
            re, im = short_transform([p[0] for p in pairs], [p[1] for p in pairs], -1.0)
            for k1 in range(32):
                c, s = twist_ref[0, k1 : k1 + 1, :], twist_ref[1, k1 : k1 + 1, :]
                target[k1, rows, :LANES] = re[k1] * c + im[k1] * s
                target[k1, rows, LANES:] = im[k1] * c - re[k1] * s
            return carry

        lax.fori_loop(0, PAD // 8, body, 0)

    def first_inverse(target):
        def body(step, carry):
            rows = pl.ds(pl.multiple_of(step * 8, 8), 8)
            res, ims = [], []
            for k1 in range(32):
                c, s = twist_ref[0, k1 : k1 + 1, :], twist_ref[1, k1 : k1 + 1, :]
                re, im = tw[k1, rows, :LANES], tw[k1, rows, LANES:]
                res.append(re * c - im * s)
                ims.append(im * c + re * s)
            re, im = short_transform(res, ims, 1.0)
            for i in range(SPEC):
                target[i, 0, rows, :] = re[i]
                target[i, 1, rows, :] = im[i]
            return carry

        lax.fori_loop(0, PAD // 8, body, 0)

    def chunks(body):
        def step(c, carry):
            body(pl.ds(c * 8, 8))
            return carry

        lax.fori_loop(0, 4, step, 0)

    def flow(source, which, index):
        def body(part):
            spectrum = dot(source[part].reshape(192, 256).astype(BF16), lane_ref[which])
            factor = mult_flow[part].reshape(192, LANES)
            scaled = jnp.concatenate([spectrum[:, :LANES] * factor, spectrum[:, LANES:] * factor], axis=1)
            tw[part] = dot(scaled.astype(BF16), lane_ref[3]).reshape(8, PAD, 256)

        chunks(body)
        first_inverse(s2.at[index])
        send_all(2 + index, lambda peer, slot: s2.at[index, peer, :, some], r2.at[index, my_slot, :, some])
        r2[index, my_slot] = s2[index, me]

    sign = jnp.where(low, 1.0, -1.0)

    def load_base(i, rows):
        value = r1[i, 0, rows, :]
        return value, pltpu.roll(value, SLAB, 1) * sign

    wait_for(recv_sem, 0, r1.at[most, pl.ds(0, 1), some])
    first_forward(load_base, tb)
    flow(tb, 0, 0)
    wait_for(recv_sem, 1, r1.at[most, pl.ds(1, 2), some])
    first_forward(lambda i, rows: (r1[i, 1, rows, :], r1[i, 2, rows, :]), tt)
    flow(tt, 0, 1)
    flow(tt, 1, 2)

    def start_spectrum(part):
        spectrum = dot(tt[part].reshape(192, 256).astype(BF16), lane_ref[2])
        decay = mult_decay[part]
        zr[part] = spectrum[:, :LANES].reshape(8, PAD, LANES) * decay
        zi[part] = spectrum[:, LANES:].reshape(8, PAD, LANES) * decay

    chunks(start_spectrum)

    def second_inverse(ref, body):
        even = ref[pl.ds(0, 16)].reshape(SIDE, LANES).astype(BF16)
        odd = ref[pl.ds(16, 16)].reshape(SIDE, LANES).astype(BF16)

        def step(c, carry):
            rows = pl.ds(pl.multiple_of(c * 256, 256), 256)
            e = dot(ti_ref[0, rows, :], even)
            o = dot(ti_ref[1, rows, :], odd)
            body(c, e + o, e - o)
            return carry

        lax.fori_loop(0, 4, step, 0)

    wait_for(recv_sem, 2, r2.at[0, most, :, some])

    def keep_base(c, lower, upper):
        base_flow[pl.ds(pl.multiple_of(c * 256, 256), 256), :] = lower
        base_flow[pl.ds(pl.multiple_of(c * 256 + HALF, 256), 256), :] = upper

    second_inverse(r2.at[0], keep_base)

    def products(b, t):
        straight = b * t
        crossed = b * pltpu.roll(t, SLAB, 1)
        near = jnp.where(low, crossed, straight)
        far = pltpu.roll(jnp.where(low, straight, crossed), SLAB, 1)
        return near + far * sign

    for index in range(2):
        wait_for(recv_sem, 3 + index, r2.at[1 + index, most, :, some])

        def multiply(c, lower, upper):
            rows = pl.ds(pl.multiple_of(c * 256, 256), 256)
            lo = products(base_flow[rows, :], lower)
            hi = products(base_flow[pl.ds(pl.multiple_of(c * 256 + HALF, 256), 256), :], upper)
            product[0, rows, :] = (lo + hi).astype(BF16)
            product[1, rows, :] = (lo - hi).astype(BF16)

        second_inverse(r2.at[1 + index], multiply)

        for parity in range(2):
            def product_rows(step, carry, parity=parity, index=index):
                rows = pl.ds(pl.multiple_of(step * 192, 192), 192)
                out = dot(tf_ref[parity, rows, :], product[parity])
                s3[index, pl.ds(parity * 16 + step * 4, 4)] = out.reshape(4, 2, PAD, LANES)
                return carry

            lax.fori_loop(0, 4, product_rows, 0)

        send_all(
            5 + index,
            lambda peer, slot, index=index: s3.at[index, slot, :, some],
            r3.at[index, me, :, some],
        )
        r3[index, me] = s3[index, my_slot]

    for index in range(2):
        wait_for(recv_sem, 5 + index, r3.at[index, most, :, some])
        first_forward(lambda i, rows, index=index: (r3[index, i, 0, rows, :], r3[index, i, 1, rows, :]), tb)

        def add_slope(part, index=index):
            spectrum = dot(tb[part].reshape(192, 256).astype(BF16), lane_ref[2])
            factor = mult_slope[part].reshape(192, LANES)
            for half, ref in ((0, zr), (1, zi)):
                terms = spectrum[:, half * LANES : (half + 1) * LANES] * factor
                slope = terms + pltpu.roll(terms, SLAB, 1)
                slope = jnp.where(low, slope, 0.0) if index == 0 else jnp.where(low, 0.0, slope)
                ref[part] = ref[part] + slope.reshape(8, PAD, LANES)

        chunks(add_slope)

    def inner(k1, carry):
        squares, crosses = carry
        re, im = zr[k1], zi[k1]
        squares = squares + (re * re + im * im) * gram_weight
        crosses = crosses + (re * pltpu.roll(re, SLAB, 1) + im * pltpu.roll(im, SLAB, 1)) * gram_weight
        return squares, crosses

    nothing = jnp.zeros((PAD, LANES), F32)
    squares, crosses = lax.fori_loop(0, 32, inner, (nothing, nothing))

    def total(x):
        return jnp.sum(jnp.sum(x, axis=0, keepdims=True), axis=1, keepdims=True)

    lane8 = lax.broadcasted_iota(jnp.int32, (8, LANES), 1)

    def spread(first, second, third):
        return jnp.where(lane8 == 0, first, jnp.where(lane8 == 1, second, jnp.where(lane8 == 2, third, 0.0)))

    g00 = total(jnp.where(low_rows, squares, 0.0))
    g11 = total(jnp.where(low_rows, 0.0, squares))
    g01 = total(jnp.where(low_rows, crosses, 0.0))
    gs[...] = spread(g00, g01, g11)
    send_all(8, lambda peer, slot: gs, gr.at[me])
    gr[me] = gs[...]

    def final_chunk(part):
        scale = jnp.broadcast_to(to_field[None], (8, PAD, LANES))
        scaled = jnp.concatenate(
            [(zr[part] * scale).reshape(192, LANES), (zi[part] * scale).reshape(192, LANES)], axis=1
        )
        tw[part] = dot(scaled.astype(BF16), lane_ref[3]).reshape(8, PAD, 256)

    chunks(final_chunk)
    first_inverse(s4)
    send_all(7, lambda peer, slot: s4.at[peer, :, some], r4.at[my_slot, :, some])
    r4[my_slot] = s4[me]

    def pick(values, index):
        return jnp.sum(jnp.where(lane8[:1] == index, values, 0.0), axis=1, keepdims=True)

    wait_for(recv_sem, 8, gr.at[most])
    gram = jnp.sum(gr[...], axis=0)[:1]
    g00, g01, g11 = pick(gram, 0), pick(gram, 1), pick(gram, 2)
    u00 = jnp.sqrt(g00)
    u01 = g01 / u00
    u11 = jnp.sqrt(g11 - u01 * u01)
    i00, i11 = 1.0 / u00, 1.0 / u11
    i01 = -(i00 * u01) / u11
    i10 = jnp.zeros_like(i00)
    ts[...] = spread(i00, i01, i11)

    def share(d, carry):
        pltpu.make_async_remote_copy(
            src_ref=ts,
            dst_ref=tr.at[seg],
            send_sem=send_sem.at[9],
            recv_sem=recv_sem.at[9],
            device_id={"tm": lax.rem(seg + d, TM)},
            device_id_type=MESH,
        ).start()
        return carry

    lax.fori_loop(1, TM, share, 0)
    tr[seg] = ts[...]
    pair = lax.broadcasted_iota(jnp.int32, (1, 2), 1)
    growth_ref[...] = jnp.where(pair == 0, jnp.log(u00), jnp.log(u11))

    wait_for(recv_sem, 9, tr.at[pl.ds(0, TM - 1)])
    one, zero = jnp.ones_like(i00), jnp.zeros_like(i00)
    end00, end01, end11 = end_ref[0, 0], end_ref[0, 1], end_ref[1, 1]
    p00, p01, p10, p11 = one, zero, zero, one
    for later in range(TM - 1, -1, -1):
        values = tr[later][:1]
        active = later >= seg
        a00 = jnp.where(active, pick(values, 0), one)
        a01 = jnp.where(active, pick(values, 1), zero)
        a11 = jnp.where(active, pick(values, 2), one)
        a10 = zero
        p00, p01, p10, p11 = (
            a00 * p00 + a01 * p10,
            a00 * p01 + a01 * p11,
            a10 * p00 + a11 * p10,
            a10 * p01 + a11 * p11,
        )
    q00, q01 = p00 * end00, p00 * end01 + p01 * end11
    q10, q11 = p10 * end00, p10 * end01 + p11 * end11
    norm0 = jnp.sqrt(q00 * q00 + q10 * q10)
    norm1 = jnp.sqrt(q01 * q01 + q11 * q11)
    c00, c10, c01, c11 = q00 / norm0, q10 / norm0, q01 / norm1, q11 / norm1
    across = lax.broadcasted_iota(jnp.int32, (2, 2), 1)
    down = lax.broadcasted_iota(jnp.int32, (2, 2), 0)
    coef_ref[0] = jnp.where(
        down == 0, jnp.where(across == 0, c00, c01), jnp.where(across == 0, c10, c11)
    )
    cov_ref[0, 0] = tang_ref[0, 0] * c00 + tang_ref[0, 1] * c10
    cov_ref[0, 1] = tang_ref[0, 0] * c01 + tang_ref[0, 1] * c11

    wait_for(recv_sem, 7, r4.at[most, :, some])
    even = r4[pl.ds(0, 16)].reshape(SIDE, LANES).T.astype(BF16)
    odd = r4[pl.ds(16, 16)].reshape(SIDE, LANES).T.astype(BF16)
    for c in range(4):
        e = dot(even, tf_ref[0, :, c * 256 : (c + 1) * 256])
        o = dot(odd, tf_ref[1, :, c * 256 : (c + 1) * 256])
        for start, value in ((c * 256, e + o), (c * 256 + HALF, e - o)):
            first, second_value = value[:SLAB], value[SLAB:]
            basis_ref[0, 0, :, start : start + 256] = first * i00 + second_value * i10
            basis_ref[0, 1, :, start : start + 256] = first * i01 + second_value * i11

    wait_for(send_sem, 0, s1.at[most, pl.ds(0, 1), some])
    wait_for(send_sem, 1, s1.at[most, pl.ds(1, 2), some])
    for index in range(3):
        wait_for(send_sem, 2 + index, s2.at[index, most, :, some])
    for index in range(2):
        wait_for(send_sem, 5 + index, s3.at[index, most, :, some])
    wait_for(send_sem, 7, s4.at[most, :, some])
    wait_for(send_sem, 8, gr.at[most])
    wait_for(send_sem, 9, tr.at[pl.ds(0, TM - 1)])


def shards(base_flow, tangents, end_matrix):
    rows = row_tables()
    tf = jnp.asarray(rows.astype(ml_dtypes.bfloat16))
    ti = jnp.asarray(np.ascontiguousarray(rows.transpose(0, 2, 1)).astype(ml_dtypes.bfloat16))
    lanes = jnp.asarray(lane_tables().astype(ml_dtypes.bfloat16))
    twist = jnp.asarray(twist_tables().astype(np.float32))
    vmem = pl.BlockSpec(memory_space=pltpu.VMEM)
    smem = pl.BlockSpec(memory_space=pltpu.SMEM)

    def buffer(*lead):
        return pltpu.VMEM(lead + (PAD, LANES), F32)

    return pl.pallas_call(
        kernel,
        out_shape=(
            jax.ShapeDtypeStruct((1, K, SLAB, NG), F32),
            jax.ShapeDtypeStruct((1, K, SLAB, NG), F32),
            jax.ShapeDtypeStruct((1, K, K), F32),
            jax.ShapeDtypeStruct((1, K), F32),
        ),
        in_specs=[vmem, vmem, smem, vmem, vmem, vmem, vmem],
        out_specs=(vmem, vmem, vmem, vmem),
        scratch_shapes=[
            buffer(SPEC, 3),
            buffer(SPEC, 3),
            buffer(3, SPEC, 2),
            buffer(3, SPEC, 2),
            buffer(2, SPEC, 2),
            buffer(2, SPEC, 2),
            buffer(SPEC, 2),
            buffer(SPEC, 2),
            pltpu.VMEM((8, LANES), F32),
            pltpu.VMEM((SPEC, 8, LANES), F32),
            pltpu.VMEM((8, LANES), F32),
            pltpu.VMEM((TM, 8, LANES), F32),
            pltpu.VMEM((32, PAD, 256), F32),
            pltpu.VMEM((32, PAD, 256), F32),
            pltpu.VMEM((32, PAD, 256), F32),
            pltpu.VMEM((4 * SLAB, HALF), BF16),
            buffer(32),
            buffer(32),
            buffer(32),
            buffer(32),
            buffer(32),
            pltpu.VMEM((NG, LANES), F32),
            pltpu.VMEM((2, HALF, LANES), BF16),
            pltpu.SemaphoreType.DMA((10,)),
            pltpu.SemaphoreType.DMA((10,)),
        ],
        compiler_params=pltpu.CompilerParams(
            collective_id=0, has_side_effects=True, vmem_limit_bytes=56 * 1024 * 1024
        ),
        cost_estimate=pl.CostEstimate(flops=12_000_000_000, bytes_accessed=12_000_000, transcendentals=0),
    )(base_flow, tangents, end_matrix, tf, ti, lanes, twist)


def solution(mesh):
    in_specs = (P("tm", "spec", None), P("tm", None, "spec", None), P())
    out_specs = (
        P("tm", None, "spec", None),
        P("tm", None, "spec", None),
        P("tm", None, None),
        P("tm", None),
    )
    return jax.shard_map(shards, mesh=mesh, in_specs=in_specs, out_specs=out_specs, check_vma=False)
```

profile of v0, /device:TPU:1, one launch (start us, length us, event | category | flops | bytes accessed | tf_op | source)
XLA Modules:
  0.0 101.8 jit_solution(727615111658554602)
XLA Ops:
  0.6 95.4 %shard_map.102 = (f32[1,2,64,2048]{3,2,1,0:T(8,128)}, f32[1,2,64,2048]{3,2,1,0:T(8,128)}, f32[1,2,2]{2,1,0:T(2,128)}, f32[1,2]{1,0:T(1,128)}) custom-call(f32[1,64,2048]{2,1,0:T(8,128)} %base_ref.1, f32[1,2,64,2048]{3,2,1,0:T(8,128)} %tang_ref.1, f32[2,2]{1,0:T(2,128)} %end_ref.1, bf16[2,768,1024]{2,1,0:T(8,128)(2,1)} %constant.8.clone.tf_ref, ...), custom_call_target="tpu_custom_call" | custom-call | flops 12000000000 | bytes 12000000 | tf_op jit(solution)/shard_map/pallas_call | solution.py:519
  96.1 0.0 copy-start
  96.1 0.0 copy-start.1
  96.1 2.3 %copy.15 = f32[1,2,64,2048]{3,2,1,0:T(8,128)} copy(f32[1,2,64,2048]{3,2,1,0:T(8,128)} %get-tuple-element.8) | data formatting | bytes 2097152
  98.4 2.3 %copy.16 = f32[1,2,64,2048]{3,2,1,0:T(8,128)} copy(f32[1,2,64,2048]{3,2,1,0:T(8,128)} %get-tuple-element.9) | data formatting | bytes 2097152
  100.7 0.0 copy-done
  100.7 0.6 copy.17
  101.3 0.0 copy-done.1
  101.3 0.5 copy.18
Async XLA Ops:
  96.1 4.6 %copy-start = (f32[1,2,2]{2,1,0:T(2,128)S(1)}, f32[1,2,2]{2,1,0:T(2,128)}, u32[]{:S(2)}) copy-start(f32[1,2,2]{2,1,0:T(2,128)} %get-tuple-element.10) | copy-start | bytes 52
  96.1 5.2 %copy-start.1 = (f32[1,2]{1,0:T(1,128)S(1)}, f32[1,2]{1,0:T(1,128)}, u32[]{:S(2)}) copy-start(f32[1,2]{1,0:T(1,128)} %get-tuple-element.11) | copy-start | bytes 28
where the time goes:
time: 102 us
  Pallas kernels  95.4 us (94%)
  local copies, waits for them, and re-layouts  5.67 us (6%)
    pallas_call x1, Pallas kernels, shards(): pl.pallas_call(kernel, out_shape=(jax.ShapeDtypeStruct((1, K, SLAB, NG),...  95.4 us
    unnamed x8, local copies, waits for them, and re-layouts  5.67 us

commit v1 on v0

--- a/solution.py
+++ b/solution.py
@@ -21,6 +21,9 @@
 PAD = 24
 LANES = 128
 SIDE = 16 * 2 * PAD
+
+RELAYED = ()
+DIRECT = ((2, 2), (1, 2), (2, 1), (3, 2), (2, 3), (2, 0), (0, 2), (1, 1), (3, 3), (1, 3), (3, 1), (1, 0), (0, 1), (3, 0), (0, 3))
 
 time_step = 0.1
 visc_scale = 15.0
@@ -112,10 +115,9 @@
     ti_ref,
     lane_ref,
     twist_ref,
-    cov_ref,
-    basis_ref,
-    coef_ref,
-    growth_ref,
+    even_ref,
+    odd_ref,
+    small_ref,
     s1,
     r1,
     s2,
@@ -139,10 +141,14 @@
     mult_decay,
     base_flow,
     product,
+    landing,
+    relay_sem,
+    forward_sem,
     send_sem,
     recv_sem,
 ):
     me = lax.axis_index("spec")
+    my_x, my_y, my_core = me // 8, lax.rem(me // 2, 4), lax.rem(me, 2)
     seg = lax.axis_index("tm")
     my_slot = lax.rem(me, 2) * 16 + me // 2
     low = lax.broadcasted_iota(jnp.int32, (1, LANES), 1) < SLAB
@@ -165,27 +171,89 @@
 
     lax.fori_loop(1, TM, greet_segment, 0)
 
+    def place(x, y, core):
+        return (lax.rem(x, 4) * 4 + lax.rem(y, 4)) * 2 + core
+
+    def slot_of(device):
+        return lax.rem(device, 2) * 16 + device // 2
+
+    def start_copy(source, target, out_sem, in_sem, device):
+        pltpu.make_async_remote_copy(
+            src_ref=source,
+            dst_ref=target,
+            send_sem=out_sem,
+            recv_sem=in_sem,
+            device_id={"spec": device},
+            device_id_type=MESH,
+        ).start()
+
+    def send_core(phase, core, source, target):
+        for number, (dx, dy) in enumerate(RELAYED):
+            peer = place(my_x + dx, my_y + dy, core)
+            start_copy(
+                source(peer, slot_of(peer)),
+                landing.at[phase, my_core * 2 + number, pl.ds(0, source(0, 0).shape[0]), pl.ds(0, ROWS)],
+                send_sem.at[phase],
+                relay_sem.at[phase],
+                place(my_x, my_y + 2, core),
+            )
+        for dx, dy in DIRECT:
+            peer = place(my_x + dx, my_y + dy, core)
+            start_copy(
+                source(peer, slot_of(peer)), target(me, my_slot), send_sem.at[phase], recv_sem.at[phase], peer
+            )
+
+    def send_other(phase, source, target):
+        peer = place(my_x, my_y, 1 - my_core)
+        start_copy(
+            source(peer, slot_of(peer)), target(me, my_slot), send_sem.at[phase], recv_sem.at[phase], peer
+        )
+
     def send_all(phase, source, target):
-        def step(d, carry):
-            peer = lax.rem(me + d, SPEC)
-            slot = lax.rem(peer, 2) * 16 + peer // 2
-            pltpu.make_async_remote_copy(
-                src_ref=source(peer, slot),
-                dst_ref=target,
-                send_sem=send_sem.at[phase],
-                recv_sem=recv_sem.at[phase],
-                device_id={"spec": peer},
-                device_id_type=MESH,
-            ).start()
+        def step(core, carry):
+            send_core(phase, core, source, target)
             return carry
 
-        lax.fori_loop(1, SPEC, step, 0)
+        lax.fori_loop(0, 2, step, 0)
+        send_other(phase, source, target)
+
+    def relay(phase, count, target):
+        wait_for(relay_sem, phase, landing.at[phase, :, pl.ds(0, count), pl.ds(0, ROWS)])
+
+        def step(core, carry):
+            origin = place(my_x, my_y + 2, core)
+            for number, (dx, dy) in enumerate(RELAYED):
+                start_copy(
+                    landing.at[phase, core * 2 + number, pl.ds(0, count), pl.ds(0, ROWS)],
+                    target(origin, slot_of(origin)),
+                    forward_sem.at[phase],
+                    recv_sem.at[phase],
+                    place(my_x + dx, my_y, my_core),
+                )
+            return carry
+
+        lax.fori_loop(0, 2, step, 0)
 
     def wait_for(sem, phase, ref):
         pltpu.make_async_copy(ref, ref, sem.at[phase]).wait()
 
     some = pl.ds(0, ROWS)
     most = pl.ds(0, SPEC - 1)
+
+    def to_base(origin, slot):
+        return r1.at[origin, pl.ds(0, 1), some]
+
+    def to_tangents(origin, slot):
+        return r1.at[origin, pl.ds(1, 2), some]
+
+    def to_flow(index):
+        return lambda origin, slot: r2.at[index, slot, :, some]
+
+    def to_slope(index):
+        return lambda origin, slot: r3.at[index, origin, :, some]
+
+    def to_evolved(origin, slot):
+        return r4.at[slot, :, some]
 
     for parity in range(2):
         def fold(half_parity=parity):
@@ -210,8 +278,8 @@
         lax.fori_loop(0, 4, spectrum_rows, 0)
 
     pl.semaphore_wait(barrier, SPEC - 1 + TM - 1)
-    send_all(0, lambda peer, slot: s1.at[slot, pl.ds(0, 1), some], r1.at[me, pl.ds(0, 1), some])
-    send_all(1, lambda peer, slot: s1.at[slot, pl.ds(1, 2), some], r1.at[me, pl.ds(1, 2), some])
+    send_all(0, lambda peer, slot: s1.at[slot, pl.ds(0, 1), some], to_base)
+    send_all(1, lambda peer, slot: s1.at[slot, pl.ds(1, 2), some], to_tangents)
     r1[me] = s1[my_slot]
 
     lane = lax.broadcasted_iota(jnp.int32, (PAD, LANES), 1)
@@ -289,7 +357,7 @@
 
         chunks(body)
         first_inverse(s2.at[index])
-        send_all(2 + index, lambda peer, slot: s2.at[index, peer, :, some], r2.at[index, my_slot, :, some])
+        send_all(2 + index, lambda peer, slot: s2.at[index, peer, :, some], to_flow(index))
         r2[index, my_slot] = s2[index, me]
 
     sign = jnp.where(low, 1.0, -1.0)
@@ -366,7 +434,7 @@
         send_all(
             5 + index,
             lambda peer, slot, index=index: s3.at[index, slot, :, some],
-            r3.at[index, me, :, some],
+            to_slope(index),
         )
         r3[index, me] = s3[index, my_slot]
 
@@ -407,7 +475,12 @@
     g11 = total(jnp.where(low_rows, 0.0, squares))
     g01 = total(jnp.where(low_rows, crosses, 0.0))
     gs[...] = spread(g00, g01, g11)
-    send_all(8, lambda peer, slot: gs, gr.at[me])
+
+    def share_gram(d, carry):
+        start_copy(gs, gr.at[me], send_sem.at[8], recv_sem.at[8], lax.rem(me + d, SPEC))
+        return carry
+
+    lax.fori_loop(1, SPEC, share_gram, 0)
     gr[me] = gs[...]
 
     def final_chunk(part):
@@ -419,8 +492,9 @@
 
     chunks(final_chunk)
     first_inverse(s4)
-    send_all(7, lambda peer, slot: s4.at[peer, :, some], r4.at[my_slot, :, some])
+    send_all(7, lambda peer, slot: s4.at[peer, :, some], to_evolved)
     r4[my_slot] = s4[me]
+
 
     def pick(values, index):
         return jnp.sum(jnp.where(lane8[:1] == index, values, 0.0), axis=1, keepdims=True)
@@ -449,9 +523,6 @@
 
     lax.fori_loop(1, TM, share, 0)
     tr[seg] = ts[...]
-    pair = lax.broadcasted_iota(jnp.int32, (1, 2), 1)
-    growth_ref[...] = jnp.where(pair == 0, jnp.log(u00), jnp.log(u11))
-
     wait_for(recv_sem, 9, tr.at[pl.ds(0, TM - 1)])
     one, zero = jnp.ones_like(i00), jnp.zeros_like(i00)
     end00, end01, end11 = end_ref[0, 0], end_ref[0, 1], end_ref[1, 1]
@@ -474,24 +545,14 @@
     norm0 = jnp.sqrt(q00 * q00 + q10 * q10)
     norm1 = jnp.sqrt(q01 * q01 + q11 * q11)
     c00, c10, c01, c11 = q00 / norm0, q10 / norm0, q01 / norm1, q11 / norm1
-    across = lax.broadcasted_iota(jnp.int32, (2, 2), 1)
-    down = lax.broadcasted_iota(jnp.int32, (2, 2), 0)
-    coef_ref[0] = jnp.where(
-        down == 0, jnp.where(across == 0, c00, c01), jnp.where(across == 0, c10, c11)
-    )
-    cov_ref[0, 0] = tang_ref[0, 0] * c00 + tang_ref[0, 1] * c10
-    cov_ref[0, 1] = tang_ref[0, 0] * c01 + tang_ref[0, 1] * c11
+    small = jnp.zeros((8, LANES), F32)
+    for number, value in enumerate((c00, c01, c10, c11, i00, i01, i10, i11, jnp.log(u00), jnp.log(u11))):
+        small = jnp.where(lane8 == number, value, small)
+    small_ref[...] = small
 
     wait_for(recv_sem, 7, r4.at[most, :, some])
-    even = r4[pl.ds(0, 16)].reshape(SIDE, LANES).T.astype(BF16)
-    odd = r4[pl.ds(16, 16)].reshape(SIDE, LANES).T.astype(BF16)
-    for c in range(4):
-        e = dot(even, tf_ref[0, :, c * 256 : (c + 1) * 256])
-        o = dot(odd, tf_ref[1, :, c * 256 : (c + 1) * 256])
-        for start, value in ((c * 256, e + o), (c * 256 + HALF, e - o)):
-            first, second_value = value[:SLAB], value[SLAB:]
-            basis_ref[0, 0, :, start : start + 256] = first * i00 + second_value * i10
-            basis_ref[0, 1, :, start : start + 256] = first * i01 + second_value * i11
+    even_ref[...] = r4[pl.ds(0, 16)].reshape(SIDE, LANES).T.astype(BF16)
+    odd_ref[...] = r4[pl.ds(16, 16)].reshape(SIDE, LANES).T.astype(BF16)
 
     wait_for(send_sem, 0, s1.at[most, pl.ds(0, 1), some])
     wait_for(send_sem, 1, s1.at[most, pl.ds(1, 2), some])
@@ -504,6 +565,43 @@
     wait_for(send_sem, 9, tr.at[pl.ds(0, TM - 1)])
 
 
+def finish(even_ref, odd_ref, small_ref, tf_ref, tang_ref, cov_ref, basis_ref, coef_ref, growth_ref, upper):
+    step = pl.program_id(0)
+    small = small_ref[:1, :]
+    lane = lax.broadcasted_iota(jnp.int32, (1, LANES), 1)
+
+    def pick(index):
+        return jnp.sum(jnp.where(lane == index, small, 0.0), axis=1, keepdims=True)
+
+    c00, c01, c10, c11, i00, i01, i10, i11, log0, log1 = [pick(number) for number in range(10)]
+
+    def write(value):
+        first, second = value[:SLAB], value[SLAB:]
+        basis_ref[0, 0] = first * i00 + second * i10
+        basis_ref[0, 1] = first * i01 + second * i11
+
+    @pl.when(step < 2)
+    def _():
+        e = dot(even_ref[...], tf_ref[0])
+        o = dot(odd_ref[...], tf_ref[1])
+        upper[step] = e - o
+        write(e + o)
+
+    @pl.when(step >= 2)
+    def _():
+        write(upper[step - 2])
+
+    cov_ref[0, 0] = tang_ref[0, 0] * c00 + tang_ref[0, 1] * c10
+    cov_ref[0, 1] = tang_ref[0, 0] * c01 + tang_ref[0, 1] * c11
+    across = lax.broadcasted_iota(jnp.int32, (2, 2), 1)
+    down = lax.broadcasted_iota(jnp.int32, (2, 2), 0)
+    coef_ref[0] = jnp.where(
+        down == 0, jnp.where(across == 0, c00, c01), jnp.where(across == 0, c10, c11)
+    )
+    pair = lax.broadcasted_iota(jnp.int32, (1, 2), 1)
+    growth_ref[...] = jnp.where(pair == 0, log0, log1)
+
+
 def shards(base_flow, tangents, end_matrix):
     rows = row_tables()
     tf = jnp.asarray(rows.astype(ml_dtypes.bfloat16))
@@ -516,16 +614,15 @@
     def buffer(*lead):
         return pltpu.VMEM(lead + (PAD, LANES), F32)
 
-    return pl.pallas_call(
+    even, odd, small = pl.pallas_call(
         kernel,
         out_shape=(
-            jax.ShapeDtypeStruct((1, K, SLAB, NG), F32),
-            jax.ShapeDtypeStruct((1, K, SLAB, NG), F32),
-            jax.ShapeDtypeStruct((1, K, K), F32),
-            jax.ShapeDtypeStruct((1, K), F32),
+            jax.ShapeDtypeStruct((LANES, SIDE), BF16),
+            jax.ShapeDtypeStruct((LANES, SIDE), BF16),
+            jax.ShapeDtypeStruct((8, LANES), F32),
         ),
         in_specs=[vmem, vmem, smem, vmem, vmem, vmem, vmem],
-        out_specs=(vmem, vmem, vmem, vmem),
+        out_specs=(vmem, vmem, vmem),
         scratch_shapes=[
             buffer(SPEC, 3),
             buffer(SPEC, 3),
@@ -550,6 +647,9 @@
             buffer(32),
             pltpu.VMEM((NG, LANES), F32),
             pltpu.VMEM((2, HALF, LANES), BF16),
+            buffer(8, 4, 2),
+            pltpu.SemaphoreType.DMA((8,)),
+            pltpu.SemaphoreType.DMA((8,)),
             pltpu.SemaphoreType.DMA((10,)),
             pltpu.SemaphoreType.DMA((10,)),
         ],
@@ -558,6 +658,30 @@
         ),
         cost_estimate=pl.CostEstimate(flops=12_000_000_000, bytes_accessed=12_000_000, transcendentals=0),
     )(base_flow, tangents, end_matrix, tf, ti, lanes, twist)
+
+    whole = lambda *shape: pl.BlockSpec(shape, lambda g: (0,) * len(shape))
+    wide = pl.BlockSpec((1, K, SLAB, 512), lambda g: (0, 0, 0, g))
+    return pl.pallas_call(
+        finish,
+        grid=(4,),
+        out_shape=(
+            jax.ShapeDtypeStruct((1, K, SLAB, NG), F32),
+            jax.ShapeDtypeStruct((1, K, SLAB, NG), F32),
+            jax.ShapeDtypeStruct((1, K, K), F32),
+            jax.ShapeDtypeStruct((1, K), F32),
+        ),
+        in_specs=[
+            whole(LANES, SIDE),
+            whole(LANES, SIDE),
+            whole(8, LANES),
+            pl.BlockSpec((2, SIDE, 512), lambda g: (0, 0, jnp.minimum(g, 1))),
+            wide,
+        ],
+        out_specs=(wide, wide, whole(1, K, K), whole(1, K)),
+        scratch_shapes=[pltpu.VMEM((2, LANES, 512), F32)],
+        compiler_params=pltpu.CompilerParams(vmem_limit_bytes=24 * 1024 * 1024),
+        cost_estimate=pl.CostEstimate(flops=400_000_000, bytes_accessed=6_500_000, transcendentals=0),
+    )(even, odd, small, tf, tangents)
 
 
 def solution(mesh):

time: 102 us -> 90.3 us (0.89)
  Pallas kernels: 95.4 us -> 86.9 us
  local copies, waits for them, and re-layouts: 5.67 us -> 2.54 us
    pallas_call x1 -> x2, Pallas kernels: 95.4 us -> 86.9 us  [the longest x1 83.8 us: shards(): pl.pallas_call(kernel, out_shape=(jax.ShapeDtypeStruct((LANES, SIDE), BF1...]
    unnamed x8 -> x10, local copies, waits for them, and re-layouts: 5.67 us -> 2.54 us
where the time goes in v1:
time: 90.3 us; the launch traced here: 90.1 us
  Pallas kernels  86.9 us (96%)
  local copies, waits for them, and re-layouts  2.54 us (3%)
    pallas_call x1, Pallas kernels, shards(): pl.pallas_call(kernel, out_shape=(jax.ShapeDtypeStruct((LANES, SIDE), BF1...  83.8 us
    pallas_call x1, Pallas kernels, shards(): pl.pallas_call(finish, grid=(4,), out_shape=(jax.ShapeDtypeStruct((1, K,...  3.07 us
    unnamed x10, local copies, waits for them, and re-layouts  2.54 us

profile of v1, /device:TPU:1, one launch (start us, length us, event | category | flops | bytes accessed | tf_op | source)
XLA Modules:
  0.0 90.1 jit_solution(4980061385454778880)
XLA Ops:
  0.6 0.0 copy-start
  0.6 0.0 copy-start.1
  0.7 83.8 %shard_map.102 = (bf16[128,768]{1,0:T(8,128)(2,1)}, bf16[128,768]{1,0:T(8,128)(2,1)}, f32[8,128]{1,0:T(8,128)}) custom-call(f32[1,64,2048]{2,1,0:T(8,128)} %base_ref.1, f32[1,2,64,2048]{3,2,1,0:T(8,128)} %tang_ref.3, f32[2,2]{1,0:T(2,128)} %end_ref.1, bf16[2,768,1024]{2,1,0:T(8,128)(2,1)} %constant.8.clone.tf_ref, ...), custom_call_target="tpu_custom_call" | custom-call | flops 12000000000 | bytes 12000000 | tf_op jit(solution)/shard_map/pallas_call | solution.py:617
  84.5 0.0 copy-done
  84.5 0.0 copy-done.1
  84.5 0.0 copy-start.2
  84.5 0.9 %copy-done.2 = bf16[128,768]{1,0:T(8,128)(2,1)S(1)} copy-done((bf16[128,768]{1,0:T(8,128)(2,1)S(1)}, bf16[128,768]{1,0:T(8,128)(2,1)}, u32[]{:S(2)}) %copy-start.2) | copy-done | bytes 196632
  85.4 0.0 copy-start.3
  85.4 0.9 %copy-done.3 = bf16[128,768]{1,0:T(8,128)(2,1)S(1)} copy-done((bf16[128,768]{1,0:T(8,128)(2,1)S(1)}, bf16[128,768]{1,0:T(8,128)(2,1)}, u32[]{:S(2)}) %copy-start.3) | copy-done | bytes 196632
  86.4 0.0 copy-start.4
  86.4 0.7 copy-done.4
  87.0 3.1 %shard_map.103 = (f32[1,2,64,2048]{3,2,1,0:T(8,128)}, f32[1,2,64,2048]{3,2,1,0:T(8,128)}, f32[1,2,2]{2,1,0:T(2,128)}, f32[1,2]{1,0:T(1,128)}) custom-call(bf16[128,768]{1,0:T(8,128)(2,1)S(1)} %copy-done.2, bf16[128,768]{1,0:T(8,128)(2,1)S(1)} %copy-done.3, f32[8,128]{1,0:T(8,128)S(1)} %copy-done.4, bf16[2,768,1024]{2,1,0:T(8,128)(2,1)S(1)} %copy-done, ...), custom_call_target="tpu_custom_call" | custom-call | flops 400000000 | bytes 6500000 | tf_op jit(solution)/shard_map/pallas_call | solution.py:664
Async XLA Ops:
  0.6 83.8 %copy-start = (bf16[2,768,1024]{2,1,0:T(8,128)(2,1)S(1)}, bf16[2,768,1024]{2,1,0:T(8,128)(2,1)}, u32[]{:S(2)}) copy-start(bf16[2,768,1024]{2,1,0:T(8,128)(2,1)} %constant.8.clone.tf_ref) | copy-start | bytes 9437188
  0.6 83.8 %copy-start.1 = (f32[1,2,64,2048]{3,2,1,0:T(8,128)S(1)}, f32[1,2,64,2048]{3,2,1,0:T(8,128)}, u32[]{:S(2)}) copy-start(f32[1,2,64,2048]{3,2,1,0:T(8,128)} %tang_ref.3) | copy-start | bytes 3145732
  84.5 0.9 %copy-start.2 = (bf16[128,768]{1,0:T(8,128)(2,1)S(1)}, bf16[128,768]{1,0:T(8,128)(2,1)}, u32[]{:S(2)}) copy-start(bf16[128,768]{1,0:T(8,128)(2,1)} %get-tuple-element.7.even_ref) | copy-start | bytes 589828
  85.4 0.9 %copy-start.3 = (bf16[128,768]{1,0:T(8,128)(2,1)S(1)}, bf16[128,768]{1,0:T(8,128)(2,1)}, u32[]{:S(2)}) copy-start(bf16[128,768]{1,0:T(8,128)(2,1)} %get-tuple-element.8.odd_ref) | copy-start | bytes 589828
  86.4 0.7 copy-start.4

commit v2 on v1

--- a/solution.py
+++ b/solution.py
@@ -22,7 +22,6 @@
 LANES = 128
 SIDE = 16 * 2 * PAD
 
-RELAYED = ()
 DIRECT = ((2, 2), (1, 2), (2, 1), (3, 2), (2, 3), (2, 0), (0, 2), (1, 1), (3, 3), (1, 3), (3, 1), (1, 0), (0, 1), (3, 0), (0, 3))
 
 time_step = 0.1
@@ -111,8 +110,8 @@
     base_ref,
     tang_ref,
     end_ref,
-    tf_ref,
-    ti_ref,
+    tf_hbm,
+    ti_hbm,
     lane_ref,
     twist_ref,
     even_ref,
@@ -141,9 +140,9 @@
     mult_decay,
     base_flow,
     product,
-    landing,
-    relay_sem,
-    forward_sem,
+    tf_ref,
+    ti_ref,
+    load_sem,
     send_sem,
     recv_sem,
 ):
@@ -152,6 +151,14 @@
     seg = lax.axis_index("tm")
     my_slot = lax.rem(me, 2) * 16 + me // 2
     low = lax.broadcasted_iota(jnp.int32, (1, LANES), 1) < SLAB
+
+    loads = [
+        pltpu.make_async_copy(source.at[parity], target.at[parity], load_sem.at[number * 2 + parity])
+        for number, (source, target) in enumerate(((tf_hbm, tf_ref), (ti_hbm, ti_ref)))
+        for parity in range(2)
+    ]
+    for load in loads:
+        load.start()
 
     barrier = pltpu.get_barrier_semaphore()
 
@@ -188,15 +195,6 @@
         ).start()
 
     def send_core(phase, core, source, target):
-        for number, (dx, dy) in enumerate(RELAYED):
-            peer = place(my_x + dx, my_y + dy, core)
-            start_copy(
-                source(peer, slot_of(peer)),
-                landing.at[phase, my_core * 2 + number, pl.ds(0, source(0, 0).shape[0]), pl.ds(0, ROWS)],
-                send_sem.at[phase],
-                relay_sem.at[phase],
-                place(my_x, my_y + 2, core),
-            )
         for dx, dy in DIRECT:
             peer = place(my_x + dx, my_y + dy, core)
             start_copy(
@@ -217,27 +215,12 @@
         lax.fori_loop(0, 2, step, 0)
         send_other(phase, source, target)
 
-    def relay(phase, count, target):
-        wait_for(relay_sem, phase, landing.at[phase, :, pl.ds(0, count), pl.ds(0, ROWS)])
-
-        def step(core, carry):
-            origin = place(my_x, my_y + 2, core)
-            for number, (dx, dy) in enumerate(RELAYED):
-                start_copy(
-                    landing.at[phase, core * 2 + number, pl.ds(0, count), pl.ds(0, ROWS)],
-                    target(origin, slot_of(origin)),
-                    forward_sem.at[phase],
-                    recv_sem.at[phase],
-                    place(my_x + dx, my_y, my_core),
-                )
-            return carry
-
-        lax.fori_loop(0, 2, step, 0)
-
     def wait_for(sem, phase, ref):
         pltpu.make_async_copy(ref, ref, sem.at[phase]).wait()
 
     some = pl.ds(0, ROWS)
+    front = pl.ds(0, 16)
+    back = pl.ds(16, ROWS - 16)
     most = pl.ds(0, SPEC - 1)
 
     def to_base(origin, slot):
@@ -249,11 +232,11 @@
     def to_flow(index):
         return lambda origin, slot: r2.at[index, slot, :, some]
 
-    def to_slope(index):
-        return lambda origin, slot: r3.at[index, origin, :, some]
-
-    def to_evolved(origin, slot):
-        return r4.at[slot, :, some]
+    def to_slope(index, rows):
+        return lambda origin, slot: r3.at[index, origin, :, rows]
+
+    def to_evolved(rows):
+        return lambda origin, slot: r4.at[slot, :, rows]
 
     for parity in range(2):
         def fold(half_parity=parity):
@@ -263,6 +246,7 @@
                 folded[index * SLAB : (index + 1) * SLAB, :] = value.astype(BF16)
 
         fold()
+        loads[parity].wait()
 
         def spectrum_rows(step, carry, parity=parity):
             rows = pl.ds(pl.multiple_of(step * 192, 192), 192)
@@ -311,7 +295,7 @@
 
     lax.fori_loop(0, 32, multipliers, 0)
 
-    def first_forward(load, target):
+    def first_forward(load, target, start=0, stop=PAD // 8):
         def body(step, carry):
             rows = pl.ds(pl.multiple_of(step * 8, 8), 8)
             pairs = [load(i, rows) for i in range(SPEC)]
@@ -322,9 +306,9 @@
                 target[k1, rows, LANES:] = im[k1] * c - re[k1] * s
             return carry
 
-        lax.fori_loop(0, PAD // 8, body, 0)
-
-    def first_inverse(target):
+        lax.fori_loop(start, stop, body, 0)
+
+    def first_inverse(target, start=0, stop=PAD // 8):
         def body(step, carry):
             rows = pl.ds(pl.multiple_of(step * 8, 8), 8)
             res, ims = [], []
@@ -339,7 +323,7 @@
                 target[i, 1, rows, :] = im[i]
             return carry
 
-        lax.fori_loop(0, PAD // 8, body, 0)
+        lax.fori_loop(start, stop, body, 0)
 
     def chunks(body):
         def step(c, carry):
@@ -395,6 +379,8 @@
 
         lax.fori_loop(0, 4, step, 0)
 
+    loads[2].wait()
+    loads[3].wait()
     wait_for(recv_sem, 2, r2.at[0, most, :, some])
 
     def keep_base(c, lower, upper):
@@ -431,27 +417,54 @@
 
             lax.fori_loop(0, 4, product_rows, 0)
 
-        send_all(
-            5 + index,
-            lambda peer, slot, index=index: s3.at[index, slot, :, some],
-            to_slope(index),
+        if index == 0:
+            send_all(5, lambda peer, slot: s3.at[0, slot, :, some], to_slope(0, some))
+        else:
+            send_all(6, lambda peer, slot: s3.at[1, slot, :, front], to_slope(1, front))
+            send_all(10, lambda peer, slot: s3.at[1, slot, :, back], to_slope(1, back))
+        r3[index, me] = s3[index, my_slot]
+
+    def slope(index, start, count):
+        rows = pl.ds(start, count)
+        first_forward(
+            lambda i, rows: (r3[index, i, 0, rows, :], r3[index, i, 1, rows, :]),
+            tb,
+            start // 8,
+            (start + count) // 8,
         )
-        r3[index, me] = s3[index, my_slot]
-
-    for index in range(2):
-        wait_for(recv_sem, 5 + index, r3.at[index, most, :, some])
-        first_forward(lambda i, rows, index=index: (r3[index, i, 0, rows, :], r3[index, i, 1, rows, :]), tb)
-
-        def add_slope(part, index=index):
-            spectrum = dot(tb[part].reshape(192, 256).astype(BF16), lane_ref[2])
-            factor = mult_slope[part].reshape(192, LANES)
+
+        def add_slope(part):
+            spectrum = dot(tb[part, rows].reshape(8 * count, 256).astype(BF16), lane_ref[2])
+            factor = mult_slope[part, rows].reshape(8 * count, LANES)
             for half, ref in ((0, zr), (1, zi)):
                 terms = spectrum[:, half * LANES : (half + 1) * LANES] * factor
-                slope = terms + pltpu.roll(terms, SLAB, 1)
-                slope = jnp.where(low, slope, 0.0) if index == 0 else jnp.where(low, 0.0, slope)
-                ref[part] = ref[part] + slope.reshape(8, PAD, LANES)
+                both = terms + pltpu.roll(terms, SLAB, 1)
+                both = jnp.where(low, both, 0.0) if index == 0 else jnp.where(low, 0.0, both)
+                ref[part, rows] = ref[part, rows] + both.reshape(8, count, LANES)
 
         chunks(add_slope)
+
+    def evolve(start, count):
+        rows = pl.ds(start, count)
+
+        def final_chunk(part):
+            scale = jnp.broadcast_to(to_field[None, start : start + count], (8, count, LANES))
+            scaled = jnp.concatenate(
+                [(ref[part, rows] * scale).reshape(8 * count, LANES) for ref in (zr, zi)], axis=1
+            )
+            tw[part, rows] = dot(scaled.astype(BF16), lane_ref[3]).reshape(8, count, 256)
+
+        chunks(final_chunk)
+        first_inverse(s4, start // 8, (start + count) // 8)
+
+    wait_for(recv_sem, 5, r3.at[0, most, :, some])
+    slope(0, 0, PAD)
+    wait_for(recv_sem, 6, r3.at[1, most, :, front])
+    slope(1, 0, 16)
+    evolve(0, 16)
+    send_all(7, lambda peer, slot: s4.at[peer, :, front], to_evolved(front))
+    wait_for(recv_sem, 10, r3.at[1, most, :, back])
+    slope(1, 16, 8)
 
     def inner(k1, carry):
         squares, crosses = carry
@@ -483,16 +496,8 @@
     lax.fori_loop(1, SPEC, share_gram, 0)
     gr[me] = gs[...]
 
-    def final_chunk(part):
-        scale = jnp.broadcast_to(to_field[None], (8, PAD, LANES))
-        scaled = jnp.concatenate(
-            [(zr[part] * scale).reshape(192, LANES), (zi[part] * scale).reshape(192, LANES)], axis=1
-        )
-        tw[part] = dot(scaled.astype(BF16), lane_ref[3]).reshape(8, PAD, 256)
-
-    chunks(final_chunk)
-    first_inverse(s4)
-    send_all(7, lambda peer, slot: s4.at[peer, :, some], to_evolved)
+    evolve(16, 8)
+    send_all(11, lambda peer, slot: s4.at[peer, :, back], to_evolved(back))
     r4[my_slot] = s4[me]
 
 
@@ -550,7 +555,8 @@
         small = jnp.where(lane8 == number, value, small)
     small_ref[...] = small
 
-    wait_for(recv_sem, 7, r4.at[most, :, some])
+    wait_for(recv_sem, 7, r4.at[most, :, front])
+    wait_for(recv_sem, 11, r4.at[most, :, back])
     even_ref[...] = r4[pl.ds(0, 16)].reshape(SIDE, LANES).T.astype(BF16)
     odd_ref[...] = r4[pl.ds(16, 16)].reshape(SIDE, LANES).T.astype(BF16)
 
@@ -558,9 +564,11 @@
     wait_for(send_sem, 1, s1.at[most, pl.ds(1, 2), some])
     for index in range(3):
         wait_for(send_sem, 2 + index, s2.at[index, most, :, some])
-    for index in range(2):
-        wait_for(send_sem, 5 + index, s3.at[index, most, :, some])
-    wait_for(send_sem, 7, s4.at[most, :, some])
+    wait_for(send_sem, 5, s3.at[0, most, :, some])
+    wait_for(send_sem, 6, s3.at[1, most, :, front])
+    wait_for(send_sem, 10, s3.at[1, most, :, back])
+    wait_for(send_sem, 7, s4.at[most, :, front])
+    wait_for(send_sem, 11, s4.at[most, :, back])
     wait_for(send_sem, 8, gr.at[most])
     wait_for(send_sem, 9, tr.at[pl.ds(0, TM - 1)])
 
@@ -610,6 +618,7 @@
     twist = jnp.asarray(twist_tables().astype(np.float32))
     vmem = pl.BlockSpec(memory_space=pltpu.VMEM)
     smem = pl.BlockSpec(memory_space=pltpu.SMEM)
+    hbm = pl.BlockSpec(memory_space=pl.ANY)
 
     def buffer(*lead):
         return pltpu.VMEM(lead + (PAD, LANES), F32)
@@ -617,11 +626,11 @@
     even, odd, small = pl.pallas_call(
         kernel,
         out_shape=(
-            jax.ShapeDtypeStruct((LANES, SIDE), BF16),
-            jax.ShapeDtypeStruct((LANES, SIDE), BF16),
-            jax.ShapeDtypeStruct((8, LANES), F32),
+            pltpu.VMEM((LANES, SIDE), BF16),
+            pltpu.VMEM((LANES, SIDE), BF16),
+            pltpu.VMEM((8, LANES), F32),
         ),
-        in_specs=[vmem, vmem, smem, vmem, vmem, vmem, vmem],
+        in_specs=[vmem, vmem, smem, hbm, hbm, vmem, vmem],
         out_specs=(vmem, vmem, vmem),
         scratch_shapes=[
             buffer(SPEC, 3),
@@ -647,11 +656,11 @@
             buffer(32),
             pltpu.VMEM((NG, LANES), F32),
             pltpu.VMEM((2, HALF, LANES), BF16),
-            buffer(8, 4, 2),
-            pltpu.SemaphoreType.DMA((8,)),
-            pltpu.SemaphoreType.DMA((8,)),
-            pltpu.SemaphoreType.DMA((10,)),
-            pltpu.SemaphoreType.DMA((10,)),
+            pltpu.VMEM((2, SIDE, HALF), BF16),
+            pltpu.VMEM((2, HALF, SIDE), BF16),
+            pltpu.SemaphoreType.DMA((4,)),
+            pltpu.SemaphoreType.DMA((12,)),
+            pltpu.SemaphoreType.DMA((12,)),
         ],
         compiler_params=pltpu.CompilerParams(
             collective_id=0, has_side_effects=True, vmem_limit_bytes=56 * 1024 * 1024

time: 90.3 us -> 84.6 us (0.937)
  Pallas kernels: 86.9 us -> 83.5 us
  local copies, waits for them, and re-layouts: 2.54 us -> 0.01 us
    pallas_call x1, Pallas kernels: 83.8 us -> 80.4 us  [shards(): pl.pallas_call(kernel, out_shape=(pltpu.VMEM((LANES, SIDE), BF16), pltpu....]
    unnamed x10 -> x4, local copies, waits for them, and re-layouts: 2.54 us -> 0.01 us
where the time goes in v2:
time: 84.6 us; the launch traced here: 84.2 us
  Pallas kernels  83.5 us (99%)
    pallas_call x1, Pallas kernels, shards(): pl.pallas_call(kernel, out_shape=(pltpu.VMEM((LANES, SIDE), BF16), pltpu....  80.4 us
    pallas_call x1, Pallas kernels, shards(): pl.pallas_call(finish, grid=(4,), out_shape=(jax.ShapeDtypeStruct((1, K,...  3.09 us

profile of v2, /device:TPU:1, one launch (start us, length us, event | category | flops | bytes accessed | tf_op | source)
XLA Modules:
  0.0 84.2 jit_solution(17335468906806045020)
XLA Ops:
  0.6 0.0 copy-start
  0.6 0.0 copy-start.1
  0.7 80.4 %shard_map.102 = (bf16[128,768]{1,0:T(8,128)(2,1)S(1)}, bf16[128,768]{1,0:T(8,128)(2,1)S(1)}, f32[8,128]{1,0:T(8,128)S(1)}) custom-call(f32[1,64,2048]{2,1,0:T(8,128)} %base_ref.1, f32[1,2,64,2048]{3,2,1,0:T(8,128)} %tang_ref.3, f32[2,2]{1,0:T(2,128)} %end_ref.1, bf16[2,768,1024]{2,1,0:T(8,128)(2,1)} %constant.8.clone.tf_hbm.tf_ref, ...), custom_call_target="tpu_custom_call" | custom-call | flops 12000000000 | bytes 12000000 | tf_op jit(solution)/shard_map/pallas_call | solution.py:626
  81.1 0.0 copy-done
  81.1 0.0 copy-done.1
  81.1 3.1 %shard_map.103 = (f32[1,2,64,2048]{3,2,1,0:T(8,128)}, f32[1,2,64,2048]{3,2,1,0:T(8,128)}, f32[1,2,2]{2,1,0:T(2,128)}, f32[1,2]{1,0:T(1,128)}) custom-call(bf16[128,768]{1,0:T(8,128)(2,1)S(1)} %get-tuple-element.7.even_ref, bf16[128,768]{1,0:T(8,128)(2,1)S(1)} %get-tuple-element.8.odd_ref, f32[8,128]{1,0:T(8,128)S(1)} %get-tuple-element.9.small_ref, ...), custom_call_target="tpu_custom_call" | custom-call | flops 400000000 | bytes 6500000 | tf_op jit(solution)/shard_map/pallas_call | solution.py:673
Async XLA Ops:
  0.6 80.4 %copy-start = (bf16[2,768,1024]{2,1,0:T(8,128)(2,1)S(1)}, bf16[2,768,1024]{2,1,0:T(8,128)(2,1)}, u32[]{:S(2)}) copy-start(bf16[2,768,1024]{2,1,0:T(8,128)(2,1)} %constant.8.clone.tf_hbm.tf_ref) | copy-start | bytes 9437188
  0.6 80.4 %copy-start.1 = (f32[1,2,64,2048]{3,2,1,0:T(8,128)S(1)}, f32[1,2,64,2048]{3,2,1,0:T(8,128)}, u32[]{:S(2)}) copy-start(f32[1,2,64,2048]{3,2,1,0:T(8,128)} %tang_ref.3) | copy-start | bytes 3145732

commit v3 on v2

--- a/solution.py
+++ b/solution.py
@@ -490,7 +490,7 @@
     gs[...] = spread(g00, g01, g11)
 
     def share_gram(d, carry):
-        start_copy(gs, gr.at[me], send_sem.at[8], recv_sem.at[8], lax.rem(me + d, SPEC))
+        start_copy(gs.at[pl.ds(0, 1)], gr.at[me, pl.ds(0, 1)], send_sem.at[8], recv_sem.at[8], lax.rem(me + d, SPEC))
         return carry
 
     lax.fori_loop(1, SPEC, share_gram, 0)
@@ -504,8 +504,8 @@
     def pick(values, index):
         return jnp.sum(jnp.where(lane8[:1] == index, values, 0.0), axis=1, keepdims=True)
 
-    wait_for(recv_sem, 8, gr.at[most])
-    gram = jnp.sum(gr[...], axis=0)[:1]
+    wait_for(recv_sem, 8, gr.at[most, pl.ds(0, 1)])
+    gram = jnp.sum(gr[:, :1, :], axis=0)
     g00, g01, g11 = pick(gram, 0), pick(gram, 1), pick(gram, 2)
     u00 = jnp.sqrt(g00)
     u01 = g01 / u00
@@ -569,7 +569,7 @@
     wait_for(send_sem, 10, s3.at[1, most, :, back])
     wait_for(send_sem, 7, s4.at[most, :, front])
     wait_for(send_sem, 11, s4.at[most, :, back])
-    wait_for(send_sem, 8, gr.at[most])
+    wait_for(send_sem, 8, gr.at[most, pl.ds(0, 1)])
     wait_for(send_sem, 9, tr.at[pl.ds(0, TM - 1)])
 
 

time: 84.6 us -> 83.2 us (0.983)
  Pallas kernels: 83.5 us -> 82.4 us
    pallas_call x1, Pallas kernels: 80.4 us -> 79.3 us  [shards(): pl.pallas_call(kernel, out_shape=(pltpu.VMEM((LANES, SIDE), BF16), pltpu....]
where the time goes in v3:
time: 83.2 us; the launch traced here: 83.1 us
  Pallas kernels  82.4 us (99%)
    pallas_call x1, Pallas kernels, shards(): pl.pallas_call(kernel, out_shape=(pltpu.VMEM((LANES, SIDE), BF16), pltpu....  79.3 us
    pallas_call x1, Pallas kernels, shards(): pl.pallas_call(finish, grid=(4,), out_shape=(jax.ShapeDtypeStruct((1, K,...  3.1 us

profile of v3, /device:TPU:1, one launch (start us, length us, event | category | flops | bytes accessed | tf_op | source)
XLA Modules:
  0.0 83.1 jit_solution(4723850216513714565)
XLA Ops:
  0.6 0.0 copy-start
  0.6 0.0 copy-start.1
  0.7 79.3 %shard_map.102 = (bf16[128,768]{1,0:T(8,128)(2,1)S(1)}, bf16[128,768]{1,0:T(8,128)(2,1)S(1)}, f32[8,128]{1,0:T(8,128)S(1)}) custom-call(f32[1,64,2048]{2,1,0:T(8,128)} %base_ref.1, f32[1,2,64,2048]{3,2,1,0:T(8,128)} %tang_ref.3, f32[2,2]{1,0:T(2,128)} %end_ref.1, bf16[2,768,1024]{2,1,0:T(8,128)(2,1)} %constant.8.clone.tf_hbm.tf_ref, ...), custom_call_target="tpu_custom_call" | custom-call | flops 12000000000 | bytes 12000000 | tf_op jit(solution)/shard_map/pallas_call | solution.py:626
  80.0 0.0 copy-done
  80.0 0.0 copy-done.1
  80.0 3.1 %shard_map.103 = (f32[1,2,64,2048]{3,2,1,0:T(8,128)}, f32[1,2,64,2048]{3,2,1,0:T(8,128)}, f32[1,2,2]{2,1,0:T(2,128)}, f32[1,2]{1,0:T(1,128)}) custom-call(bf16[128,768]{1,0:T(8,128)(2,1)S(1)} %get-tuple-element.7.even_ref, bf16[128,768]{1,0:T(8,128)(2,1)S(1)} %get-tuple-element.8.odd_ref, f32[8,128]{1,0:T(8,128)S(1)} %get-tuple-element.9.small_ref, ...), custom_call_target="tpu_custom_call" | custom-call | flops 400000000 | bytes 6500000 | tf_op jit(solution)/shard_map/pallas_call | solution.py:673
Async XLA Ops:
  0.6 79.3 %copy-start = (bf16[2,768,1024]{2,1,0:T(8,128)(2,1)S(1)}, bf16[2,768,1024]{2,1,0:T(8,128)(2,1)}, u32[]{:S(2)}) copy-start(bf16[2,768,1024]{2,1,0:T(8,128)(2,1)} %constant.8.clone.tf_hbm.tf_ref) | copy-start | bytes 9437188
  0.6 79.3 %copy-start.1 = (f32[1,2,64,2048]{3,2,1,0:T(8,128)S(1)}, f32[1,2,64,2048]{3,2,1,0:T(8,128)}, u32[]{:S(2)}) copy-start(f32[1,2,64,2048]{3,2,1,0:T(8,128)} %tang_ref.3) | copy-start | bytes 3145732

commit v4 on v3

--- a/solution.py
+++ b/solution.py
@@ -517,8 +517,8 @@
 
     def share(d, carry):
         pltpu.make_async_remote_copy(
-            src_ref=ts,
-            dst_ref=tr.at[seg],
+            src_ref=ts.at[pl.ds(0, 1)],
+            dst_ref=tr.at[seg, pl.ds(0, 1)],
             send_sem=send_sem.at[9],
             recv_sem=recv_sem.at[9],
             device_id={"tm": lax.rem(seg + d, TM)},
@@ -528,12 +528,12 @@
 
     lax.fori_loop(1, TM, share, 0)
     tr[seg] = ts[...]
-    wait_for(recv_sem, 9, tr.at[pl.ds(0, TM - 1)])
+    wait_for(recv_sem, 9, tr.at[pl.ds(0, TM - 1), pl.ds(0, 1)])
     one, zero = jnp.ones_like(i00), jnp.zeros_like(i00)
     end00, end01, end11 = end_ref[0, 0], end_ref[0, 1], end_ref[1, 1]
     p00, p01, p10, p11 = one, zero, zero, one
     for later in range(TM - 1, -1, -1):
-        values = tr[later][:1]
+        values = tr[later, :1, :]
         active = later >= seg
         a00 = jnp.where(active, pick(values, 0), one)
         a01 = jnp.where(active, pick(values, 1), zero)
@@ -570,7 +570,7 @@
     wait_for(send_sem, 7, s4.at[most, :, front])
     wait_for(send_sem, 11, s4.at[most, :, back])
     wait_for(send_sem, 8, gr.at[most, pl.ds(0, 1)])
-    wait_for(send_sem, 9, tr.at[pl.ds(0, TM - 1)])
+    wait_for(send_sem, 9, tr.at[pl.ds(0, TM - 1), pl.ds(0, 1)])
 
 
 def finish(even_ref, odd_ref, small_ref, tf_ref, tang_ref, cov_ref, basis_ref, coef_ref, growth_ref, upper):
@@ -588,16 +588,16 @@
         basis_ref[0, 0] = first * i00 + second * i10
         basis_ref[0, 1] = first * i01 + second * i11
 
-    @pl.when(step < 2)
+    @pl.when(step == 0)
     def _():
         e = dot(even_ref[...], tf_ref[0])
         o = dot(odd_ref[...], tf_ref[1])
-        upper[step] = e - o
+        upper[...] = e - o
         write(e + o)
 
-    @pl.when(step >= 2)
+    @pl.when(step == 1)
     def _():
-        write(upper[step - 2])
+        write(upper[...])
 
     cov_ref[0, 0] = tang_ref[0, 0] * c00 + tang_ref[0, 1] * c10
     cov_ref[0, 1] = tang_ref[0, 0] * c01 + tang_ref[0, 1] * c11
@@ -669,10 +669,10 @@
     )(base_flow, tangents, end_matrix, tf, ti, lanes, twist)
 
     whole = lambda *shape: pl.BlockSpec(shape, lambda g: (0,) * len(shape))
-    wide = pl.BlockSpec((1, K, SLAB, 512), lambda g: (0, 0, 0, g))
+    wide = pl.BlockSpec((1, K, SLAB, HALF), lambda g: (0, 0, 0, g))
     return pl.pallas_call(
         finish,
-        grid=(4,),
+        grid=(2,),
         out_shape=(
             jax.ShapeDtypeStruct((1, K, SLAB, NG), F32),
             jax.ShapeDtypeStruct((1, K, SLAB, NG), F32),
@@ -683,11 +683,11 @@
             whole(LANES, SIDE),
             whole(LANES, SIDE),
             whole(8, LANES),
-            pl.BlockSpec((2, SIDE, 512), lambda g: (0, 0, jnp.minimum(g, 1))),
+            whole(2, SIDE, HALF),
             wide,
         ],
         out_specs=(wide, wide, whole(1, K, K), whole(1, K)),
-        scratch_shapes=[pltpu.VMEM((2, LANES, 512), F32)],
+        scratch_shapes=[pltpu.VMEM((LANES, HALF), F32)],
         compiler_params=pltpu.CompilerParams(vmem_limit_bytes=24 * 1024 * 1024),
         cost_estimate=pl.CostEstimate(flops=400_000_000, bytes_accessed=6_500_000, transcendentals=0),
     )(even, odd, small, tf, tangents)

time: 83.2 us -> 82 us (0.986)
  Pallas kernels: 82.4 us -> 81.2 us
    pallas_call x1, Pallas kernels: 3.1 us -> 2.17 us  [shards(): pl.pallas_call(finish, grid=(2,), out_shape=(jax.ShapeDtypeStruct((1, K,...]
where the time goes in v4:
time: 82 us; the launch traced here: 81.9 us
  Pallas kernels  81.2 us (99%)
    pallas_call x1, Pallas kernels, shards(): pl.pallas_call(kernel, out_shape=(pltpu.VMEM((LANES, SIDE), BF16), pltpu....  79.1 us
    pallas_call x1, Pallas kernels, shards(): pl.pallas_call(finish, grid=(2,), out_shape=(jax.ShapeDtypeStruct((1, K,...  2.17 us

profile of v4, /device:TPU:1, one launch (start us, length us, event | category | flops | bytes accessed | tf_op | source)
XLA Modules:
  0.0 81.9 jit_solution(10969372993586725719)
XLA Ops:
  0.6 0.0 copy-start
  0.6 0.0 copy-start.1
  0.7 79.1 %shard_map.102 = (bf16[128,768]{1,0:T(8,128)(2,1)S(1)}, bf16[128,768]{1,0:T(8,128)(2,1)S(1)}, f32[8,128]{1,0:T(8,128)S(1)}) custom-call(f32[1,64,2048]{2,1,0:T(8,128)} %base_ref.1, f32[1,2,64,2048]{3,2,1,0:T(8,128)} %tang_ref.3, f32[2,2]{1,0:T(2,128)} %end_ref.1, bf16[2,768,1024]{2,1,0:T(8,128)(2,1)} %constant.8.clone.tf_hbm.tf_ref, ...), custom_call_target="tpu_custom_call" | custom-call | flops 12000000000 | bytes 12000000 | tf_op jit(solution)/shard_map/pallas_call | solution.py:626
  79.7 0.0 copy-done
  79.7 0.0 copy-done.1
  79.7 2.2 %shard_map.103 = (f32[1,2,64,2048]{3,2,1,0:T(8,128)}, f32[1,2,64,2048]{3,2,1,0:T(8,128)}, f32[1,2,2]{2,1,0:T(2,128)}, f32[1,2]{1,0:T(1,128)}) custom-call(bf16[128,768]{1,0:T(8,128)(2,1)S(1)} %get-tuple-element.7.even_ref, bf16[128,768]{1,0:T(8,128)(2,1)S(1)} %get-tuple-element.8.odd_ref, f32[8,128]{1,0:T(8,128)S(1)} %get-tuple-element.9.small_ref, ...), custom_call_target="tpu_custom_call" | custom-call | flops 400000000 | bytes 6500000 | tf_op jit(solution)/shard_map/pallas_call | solution.py:673
Async XLA Ops:
  0.6 79.1 %copy-start = (bf16[2,768,1024]{2,1,0:T(8,128)(2,1)S(1)}, bf16[2,768,1024]{2,1,0:T(8,128)(2,1)}, u32[]{:S(2)}) copy-start(bf16[2,768,1024]{2,1,0:T(8,128)(2,1)} %constant.8.clone.tf_hbm.tf_ref) | copy-start | bytes 9437188
  0.6 79.1 %copy-start.1 = (f32[1,2,64,2048]{3,2,1,0:T(8,128)S(1)}, f32[1,2,64,2048]{3,2,1,0:T(8,128)}, u32[]{:S(2)}) copy-start(f32[1,2,64,2048]{3,2,1,0:T(8,128)} %tang_ref.3) | copy-start | bytes 3145732
